TPU v7x, 512 devices: a whole 4x8x8 slice. The times are simulated.
512 devices in a mesh: row: 32 (over x, z_lo, core), col: 16 (over y, z_hi).
Axes of the slice: x: 4, y: 8, z: 8 (z_hi: 2, z_lo: 4; z = z_hi * 4 + z_lo), core: 2. Of those that a mesh axis runs over, the one named last changes fastest.
Arguments:
- tokens: bfloat16 [512, 16384], P('col', 'row'), may hold values from -6 to 6
- gate_weight: bfloat16 [16384, 26624], P('row', 'col'), may hold values from -0.046875 to 0.046875
- up_weight: bfloat16 [16384, 26624], P('row', 'col'), may hold values from -0.046875 to 0.046875
- down_weight: bfloat16 [26624, 16384], P('col', 'row'), may hold values from -0.0390625 to 0.0390625
- adapter_gate_a: bfloat16 [16384, 64], P('row', 'col'), may hold values from -0.75 to 0.75
- adapter_gate_b: bfloat16 [64, 26624], P('row', 'col'), may hold values from -0.01171875 to 0.01171875
- adapter_up_a: bfloat16 [16384, 64], P('row', 'col'), may hold values from -0.75 to 0.75
- adapter_up_b: bfloat16 [64, 26624], P('row', 'col'), may hold values from -0.01171875 to 0.01171875
Outputs:
- mixed: bfloat16 [512, 16384], P('col', 'row')
All inputs are finite; a program needn't handle non-finite values.
Results may differ from a plain program's by a relative error of at most 0.02.
Values may be sent and summed in bfloat16 or wider, within the bound.
A program may use at most 128 MiB of HBM per device.

v0:
```python
import jax
import jax.numpy as jnp
from jax import lax
from jax.sharding import PartitionSpec as P

adapter_scale = 2.0


def per_device(
    tokens,
    gate_weight,
    up_weight,
    down_weight,
    adapter_gate_a,
    adapter_gate_b,
    adapter_up_a,
    adapter_up_b,
):
    second_gate, second_up = (
        lax.all_gather(adapter_gate_b, "row", axis=0, tiled=True),
        lax.all_gather(adapter_up_b, "row", axis=0, tiled=True),
    )
    first_gate, first_up = (
        lax.all_gather(adapter_gate_a, "col", axis=1, tiled=True),
        lax.all_gather(adapter_up_a, "col", axis=1, tiled=True),
    )
    gate_delta = adapter_scale * jnp.dot(
        first_gate, second_gate, preferred_element_type=jnp.float32
    )
    up_delta = adapter_scale * jnp.dot(first_up, second_up, preferred_element_type=jnp.float32)
    gate_merged = (gate_weight.astype(jnp.float32) + gate_delta).astype(jnp.bfloat16)
    up_merged = (up_weight.astype(jnp.float32) + up_delta).astype(jnp.bfloat16)
    features = lax.all_gather(tokens, "col", axis=0, tiled=True)
    gate_part = jnp.dot(features, gate_merged, preferred_element_type=jnp.float32)
    up_part = jnp.dot(features, up_merged, preferred_element_type=jnp.float32)
    summed = lax.psum_scatter(
        jnp.stack([gate_part, up_part], 1), "row", scatter_dimension=0, tiled=True
    )
    hidden = (jax.nn.silu(summed[:, 0]) * summed[:, 1]).astype(jnp.bfloat16)
    output_terms = jnp.dot(
        lax.all_gather(hidden, "row", axis=0, tiled=True),
        down_weight,
        preferred_element_type=jnp.float32,
    )
    return lax.psum_scatter(
        output_terms.astype(jnp.bfloat16), "col", scatter_dimension=0, tiled=True
    )


def solution(mesh):
    placed = (
        P("col", "row"),
        P("row", "col"),
        P("row", "col"),
        P("col", "row"),
        P("row", "col"),
        P("row", "col"),
        P("row", "col"),
        P("row", "col"),
    )
    return jax.shard_map(
        per_device, mesh=mesh, in_specs=placed, out_specs=P("col", "row"), check_vma=False
    )
```

profile of v0, /device:TPU:1, one launch (start us, length us, event | category | flops | bytes accessed | tf_op | source)
XLA Modules:
  0.0 867.6 jit_solution(6500678489178948242)
XLA Ops:
  6.5 0.0 copy-start
  6.5 0.0 all-reduce.3.cloned.1.call-start
  6.5 55.4 %all_gather.20 = bf16[512,512]{1,0:T(8,128)(2,1)S(1)} all-gather(bf16[32,512]{1,0:T(8,128)(2,1)} %param.8), channel_id=1, replica_groups=mesh['row'=32,'col'=16] {'col'}, dimensions={0}, use_global_device_ids=true | all-gather | bytes 557056 | tf_op jit(solution)/shard_map/all_gather | solution.py:33
  62.0 52.2 %all-gather.3 = bf16[32,2,1664]{2,1,0:T(2,128)(2,1)S(1)} all-gather(bf16[1,2,1664]{2,1,0:T(2,128)(2,1)} %bitcast.33), channel_id=1, replica_groups=mesh['row'=32,'col'=16] {'row'}, dimensions={0}, use_global_device_ids=true | all-gather | bytes 219648 | tf_op jit(solution)/shard_map/all_gather | solution.py:21
  114.1 0.1 reshape.7
  114.2 39.5 %all-gather.2 = bf16[16,4,512]{2,1,0:T(4,128)(2,1)S(1)} all-gather(bf16[1,4,512]{2,1,0:T(4,128)(2,1)} %bitcast.35), channel_id=1, replica_groups=mesh['row'=32,'col'=16] {'col'}, dimensions={0}, use_global_device_ids=true | all-gather | bytes 69632 | tf_op jit(solution)/shard_map/all_gather | solution.py:25
  153.7 47.3 %all-gather.1 = bf16[32,2,1664]{2,1,0:T(2,128)(2,1)S(1)} all-gather(bf16[1,2,1664]{2,1,0:T(2,128)(2,1)} %bitcast.34), channel_id=1, replica_groups=mesh['row'=32,'col'=16] {'row'}, dimensions={0}, use_global_device_ids=true | all-gather | bytes 219648 | tf_op jit(solution)/shard_map/all_gather | solution.py:20
  201.1 0.1 reshape.3
  201.2 44.4 %all-gather = bf16[16,4,512]{2,1,0:T(4,128)(2,1)S(1)} all-gather(bf16[1,4,512]{2,1,0:T(4,128)(2,1)} %bitcast.36), channel_id=1, replica_groups=mesh['row'=32,'col'=16] {'col'}, dimensions={0}, use_global_device_ids=true | all-gather | bytes 69632 | tf_op jit(solution)/shard_map/all_gather | solution.py:24
  245.6 4.8 convolution_bitcast_fusion
  250.3 4.8 convolution_bitcast_fusion.1
  255.1 6.6 pad_maximum_fusion
  261.7 11.1 %copy.9 = f32[512,2,1664]{2,1,0:T(2,128)} copy(f32[512,2,1664]{0,2,1:T(8,128)} %pad_maximum_fusion) | data formatting | bytes 13631488 | tf_op jit(solution)/shard_map/stack | solution.py:37
  272.7 0.0 all-reduce.3.cloned.1.call-update
  272.8 0.0 all-gather.6.cloned.1.call-start
  272.8 1.3 dynamic-slice
  274.7 304.6 %all-reduce.3.cloned.1.call-done = f32[512,2,1664]{2,1,0:T(2,128)} async-done(((f32[512,2,1664]{2,1,0:T(2,128)}), f32[512,2,1664]{2,1,0:T(2,128)}) %all-reduce.3.cloned.1.call-update) | async-done | bytes 6815760
  579.4 1.2 constant_dynamic-slice_fusion
  580.6 0.7 fusion
  581.2 0.0 all-gather.6.cloned.1.call-update
  581.3 0.0 reduce-scatter.2.cloned.1.call-start
  581.3 62.4 %all-gather.6.cloned.1.call-done = bf16[512,1664]{1,0:T(8,128)(2,1)} async-done(((bf16[16,1664]{1,0:T(8,128)(2,1)}), bf16[512,1664]{1,0:T(8,128)(2,1)}) %all-gather.6.cloned.1.call-update) | async-done | bytes 1703952 | tf_op jit(solution)/shard_map/all_gather | solution.py:41
  643.7 0.0 copy-done
  643.7 3.4 convolution_convert_fusion
  647.1 0.0 reduce-scatter.2.cloned.1.call-update
  647.1 214.0 %reduce-scatter.2.cloned.1.call-done = bf16[32,512]{1,0:T(8,128)(2,1)} async-done(((bf16[512,512]{1,0:T(8,128)(2,1)}), bf16[32,512]{1,0:T(8,128)(2,1)}) %reduce-scatter.2.cloned.1.call-update) | async-done | bytes 32784 | tf_op jit(solution)/shard_map/reduce_scatter | solution.py:45
  (2 shorter events, 0.0 us)
Async XLA Ops:
  6.5 637.2 %copy-start = (bf16[1664,512]{1,0:T(8,128)(2,1)S(1)}, bf16[1664,512]{1,0:T(8,128)(2,1)}, u32[]{:S(2)}) copy-start(bf16[1664,512]{1,0:T(8,128)(2,1)} %param.11) | copy-start | bytes 5111812
  6.5 572.8 %all-reduce.3.cloned.1.call-start = ((), (), s32[]{:S(2)}) async-start(), calls=%async_computation.3 | async-start | bytes 13631488
  272.8 370.9 %all-gather.6.cloned.1.call-start = ((), (), s32[]{:S(2)}) async-start(), calls=%async_computation.1 | async-start | bytes 1757184 | tf_op jit(solution)/shard_map/all_gather | solution.py:41
  581.3 279.8 %reduce-scatter.2.cloned.1.call-start = ((), (), s32[]{:S(2)}) async-start(), calls=%async_computation.2 | async-start | bytes 557056 | tf_op jit(solution)/shard_map/reduce_scatter | solution.py:45
Sparse Core Ops, SparseCore 0:
  272.9 306.4 all-reduce.2
  581.7 61.9 all-gather.5
  648.8 212.2 reduce-scatter.1
where the time goes:
time: 872 us; the launch traced here: 868 us
  waiting for transfers between devices  581 us (67%)
  blocking collectives  239 us (27%)
  local copies, waits for them, and re-layouts  13.8 us (2%)
  between operations  13.8 us (2%)
  matrix products  12.9 us (1%)
    unnamed x4, waiting for transfers between devices  305 us
    reduce_scatter x1, waiting for transfers between devices, per_device(): lax.psum_scatter(output_terms.astype(jnp.bfloat16), 'col', scatter_dimens...  214 us
    all_gather x1, waiting for transfers between devices, per_device(): lax.all_gather(hidden, 'row', axis=0, tiled=True)  62.4 us
    all_gather x1, blocking collectives, per_device(): features = lax.all_gather(tokens, 'col', axis=0, tiled=True)  55.4 us
    all_gather x1, blocking collectives, per_device(): lax.all_gather(adapter_up_b, 'row', axis=0, tiled=True)  52.2 us
    all_gather x1, blocking collectives, per_device(): lax.all_gather(adapter_gate_b, 'row', axis=0, tiled=True)  47.3 us
    all_gather x1, blocking collectives, per_device(): lax.all_gather(adapter_gate_a, 'col', axis=1, tiled=True)  44.4 us
    all_gather x1, blocking collectives, per_device(): lax.all_gather(adapter_up_a, 'col', axis=1, tiled=True)  39.5 us
  transfers between devices with their start and end apart: 3, of which 3 were waited for; matrix products, arithmetic and copies ran while one was open for 0% of the time, Pallas kernels for 0%

commit v1 on v0

v1 whole, which is shorter than its diff:
```python
import jax
import jax.numpy as jnp
from jax import lax
from jax.experimental import pallas as pl
from jax.experimental.pallas import tpu as pltpu
from jax.sharding import PartitionSpec as P

FEAT = 512
UNITS = 1664
RANKS = 128
WIDE = UNITS + RANKS
OUT = 512
MESH = pl.DeviceIdType.MESH
F32 = jnp.float32
BF16 = jnp.bfloat16


def kernel(
    tok_hbm, gw_hbm, uw_hbm, dw_hbm, ag_hbm, bg_hbm, au_hbm, bu_hbm,
    o_ref,
    gw, uw, dw, ag, au, bg, bu,
    tok, first, second, second_flat,
    part, from_core, x1_out, x1_in, x2_out, x2_in, z_out, z_in,
    hid, hid_flat, out_terms, out_in, last_out, last_in,
    local_sem, send_sem, recv_sem,
):
    row, col = lax.axis_index("row"), lax.axis_index("col")
    x, z, core = row // 8, (row // 2) % 4, row % 2
    y, zh = col // 2, col % 2

    def device(x=x, z=z, core=core, y=y, zh=zh):
        return ((x * 4 + z) * 2 + core, y * 2 + zh)

    other = 1 - core
    ring_a = device(x=x + 1 - 2 * (x % 2))
    ring_b = device(x=3 - x)
    bit_b = x // 2
    bit_a = (x % 2 + bit_b) % 2
    far_x = device(x=(x + 2) % 4)
    core_peer = device(core=other)
    zh_peer = device(zh=1 - zh)
    y_peers = [device(y=(y + k) % 8) for k in range(1, 8)]
    z_peers = [device(z=(z + k) % 4) for k in range(1, 4)]

    def fetch(src, dst, n):
        copy = pltpu.make_async_copy(src, dst, local_sem.at[n])
        copy.start()
        return copy

    small = [
        fetch(ag_hbm, ag, 0), fetch(au_hbm, au, 1), fetch(bg_hbm, bg, 2), fetch(bu_hbm, bu, 3),
    ]
    own_tokens = fetch(tok_hbm, tok.at[zh, y], 4)
    weights = [fetch(gw_hbm, gw, 5), fetch(uw_hbm, uw, 6)]
    down = fetch(dw_hbm, dw, 7)

    barrier = pltpu.get_barrier_semaphore()
    partners = [ring_a, ring_b, far_x, core_peer, zh_peer] + y_peers + z_peers
    for peer in partners:
        pl.semaphore_signal(barrier, inc=1, device_id=peer, device_id_type=MESH)

    for copy in small:
        copy.wait()
    a_g, a_u = ag[...].astype(F32), au[...].astype(F32)
    first[col] = jnp.concatenate([a_g[0:2], a_u[0:2], a_g[2:4], a_u[2:4]], 0).astype(BF16)
    b_pair = jnp.concatenate(
        [bg[...].astype(F32), bu[...].astype(F32), jnp.zeros((4, UNITS), F32)], 0
    )
    slot_b = core * 16 + x * 4 + z
    second[slot_b] = b_pair.astype(BF16)
    own_tokens.wait()
    pl.semaphore_wait(barrier, len(partners))

    started = []

    def send(src, dst, peer):
        n = len(started)
        copy = pltpu.make_async_remote_copy(
            src_ref=src, dst_ref=dst, send_sem=send_sem.at[n], recv_sem=recv_sem.at[n],
            device_id=peer, device_id_type=MESH,
        )
        copy.start()
        started.append(copy)
        return copy

    def arrived(copies):
        for copy in copies:
            copy.wait_recv()

    mine, theirs = tok.at[zh, y], tok.at[1 - zh, y]
    a_mine, a_theirs = first.at[col], first.at[y * 2 + 1 - zh]
    zh_in = [send(a_mine, a_mine, zh_peer), send(mine, mine, zh_peer)]
    tok_in = [[], []]
    a_in = []
    for peer in y_peers:
        a_in.append(send(a_mine, a_mine, peer))
    for peer in y_peers:
        tok_in[0].append(send(mine, mine, peer))
    b_in = [send(second.at[slot_b], second.at[slot_b], peer) for peer in z_peers]

    arrived(zh_in)
    for peer in y_peers:
        a_in.append(send(a_theirs, a_theirs, peer))
    for peer in y_peers:
        tok_in[1].append(send(theirs, theirs, peer))
    arrived(b_in)
    b_x = second.at[pl.ds(core * 16 + x * 4, 4)]
    b_in = [send(b_x, b_x, peer) for peer in (ring_a, ring_b, far_x)]

    lane = lax.broadcasted_iota(jnp.int32, (128, RANKS), 1) % 4
    gate_lane = lane < 2

    def project(q, half):
        side = zh if q == 0 else 1 - zh
        x_blk = tok[side, pl.ds(half * 4, 4)].reshape(128, FEAT)

        def paired(g, u):
            pair = jnp.stack([g.reshape(16, 8, 128), u.reshape(16, 8, 128)], 1)
            return pair.reshape(16, 16, 128).astype(BF16)

        def tile(t, carry):
            at = pl.multiple_of(t * 128, 128)
            w = jnp.concatenate([gw[:, pl.ds(at, 128)], uw[:, pl.ds(at, 128)]], 1)
            both = jnp.dot(x_blk, w, preferred_element_type=F32)
            part[q, half, :, :, pl.ds(at, 128)] = paired(both[:, :128], both[:, 128:])
            return carry

        lax.fori_loop(0, UNITS // 128, tile, 0)
        a_all = first[...].astype(F32).reshape(RANKS, FEAT).astype(BF16)
        ranks = lax.dot_general(
            x_blk, a_all, (((1,), (1,)), ((), ())), preferred_element_type=F32
        )
        part[q, half, :, :, UNITS:WIDE] = paired(
            jnp.where(gate_lane, ranks, 0.0), jnp.where(gate_lane, 0.0, ranks)
        )

    def sum_groups(n, terms, dst):
        def group(i, carry):
            total = terms[0](i).astype(F32)
            for term in terms[1:]:
                total = total + term(i).astype(F32)
            dst[i] = total.astype(BF16)
            return carry

        lax.fori_loop(0, n, group, 0)

    split = ((bit_a, bit_b), (bit_b, bit_a))
    first_peer, second_peer = (ring_a, ring_b), (ring_b, ring_a)
    core_in, x1, x2, z_arr, zg, xg1, xg2, core_g = ([None, None] for _ in range(8))
    y_in = [None, None]

    def step_project(q):
        arrived(tok_in[q])
        if q == 0:
            for copy in weights:
                copy.wait()
            arrived(a_in)
        project(q, other)
        core_in[q] = [send(part.at[q, other], from_core.at[q], core_peer)]
        project(q, core)

    def step_x1(q):
        arrived(core_in[q])
        x1[q] = []
        for h in (0, 1):
            base = h * 8 + (1 - split[h][0]) * 4
            sum_groups(
                4,
                [lambda i: part[q, core, base + i], lambda i: from_core[q, base + i]],
                x1_out.at[q, h],
            )
            x1[q].append(send(x1_out.at[q, h], x1_in.at[q, h], first_peer[h]))

    def step_x2(q):
        x2[q] = []
        for h in (0, 1):
            arrived(x1[q][h : h + 1])
            s = 1 - split[h][1]
            base = h * 8 + split[h][0] * 4 + s * 2
            sum_groups(
                2,
                [
                    lambda i: part[q, core, base + i],
                    lambda i: from_core[q, base + i],
                    lambda i: x1_in[q, h, s * 2 + i],
                ],
                x2_out.at[q, h],
            )
            x2[q].append(send(x2_out.at[q, h], x2_in.at[q, h], second_peer[h]))

    def kept_terms(q, k):
        h, low = k // 2, k % 2
        p = jnp.where(h == 0, bit_a, bit_b)
        s = jnp.where(h == 0, bit_b, bit_a)
        base = h * 8 + p * 4 + s * 2 + low
        return (
            part[q, core, base].astype(F32)
            + from_core[q, base].astype(F32)
            + x1_in[q, h, s * 2 + low].astype(F32)
            + x2_in[q, h, low].astype(F32)
        )

    def step_z(q):
        arrived(x2[q])
        z_arr[q] = []
        for k in range(1, 4):
            owner = (z + k) % 4
            z_out[q, k] = kept_terms(q, owner).astype(BF16)
            z_arr[q].append(send(z_out.at[q, k], z_in.at[q, k], z_peers[k - 1]))

    def own_slot():
        h, low = z // 2, z % 2
        p = jnp.where(h == 0, bit_a, bit_b)
        s = jnp.where(h == 0, bit_b, bit_a)
        return h * 8 + p * 4 + s * 2 + low

    def step_hidden(q):
        total = kept_terms(q, z)
        arrived(z_arr[q])
        for k in range(1, 4):
            total = total + z_in[q, k].astype(F32)
        k_at = lax.broadcasted_iota(jnp.int32, (RANKS, 256), 0)
        s_at = lax.broadcasted_iota(jnp.int32, (RANKS, 256), 1)
        r_of = k_at // 4
        meets = ((r_of % 2) * 16 + r_of // 2) * 8 + k_at % 4 == s_at
        spread = jnp.where(meets, 2.0, 0.0).astype(BF16)
        ranks = jnp.dot(
            total[:, UNITS:].astype(BF16), spread, preferred_element_type=F32
        ).astype(BF16)
        both = total[:, :UNITS] + jnp.dot(
            ranks, second_flat[...], preferred_element_type=F32
        )
        gate, up = both[:8], both[8:]
        slot = own_slot()
        hid[q, core, slot] = (gate / (1.0 + jnp.exp(-gate)) * up).astype(BF16)
        ref = hid.at[q, core, slot]
        zg[q] = [send(ref, ref, peer) for peer in z_peers]

    def step_xg1(q):
        arrived(zg[q])
        xg1[q] = []
        for h in (0, 1):
            ref = hid.at[q, core, pl.ds(h * 8 + split[h][0] * 4 + split[h][1] * 2, 2)]
            xg1[q].append(send(ref, ref, second_peer[h]))

    def step_xg2(q):
        xg2[q] = []
        for h in (0, 1):
            arrived(xg1[q][h : h + 1])
            ref = hid.at[q, core, pl.ds(h * 8 + split[h][0] * 4, 4)]
            xg2[q].append(send(ref, ref, first_peer[h]))

    def step_core_g(q):
        arrived(xg2[q])
        ref = hid.at[q, core]
        core_g[q] = [send(ref, ref, core_peer)]

    def down_half(q, half):
        def flat(i, carry):
            two = hid[q, half, pl.ds(i * 2, 2)].astype(F32).reshape(16, UNITS)
            hid_flat[pl.ds(pl.multiple_of(i * 16, 16), 16), :] = two.astype(BF16)
            return carry

        lax.fori_loop(0, 8, flat, 0)
        for n in range(2):
            at = n * 256
            terms = jnp.dot(hid_flat[...], dw[:, at : at + 256], preferred_element_type=F32)
            out_terms[q, pl.ds(half * 4, 4), :, at : at + 256] = terms.astype(BF16).reshape(
                4, 32, 256
            )

    def step_down(q):
        if q == 0:
            down.wait()
        down_half(q, core)
        arrived(core_g[q])
        down_half(q, other)
        y_in[q] = []
        for k in range(1, 8):
            y_in[q].append(
                send(out_terms.at[q, (y + k) % 8], out_in.at[q, k], y_peers[k - 1])
            )

    def y_sum(q):
        arrived(y_in[q])
        total = out_terms[q, y].astype(F32)
        for k in range(1, 8):
            total = total + out_in[q, k].astype(F32)
        return total

    step_project(0)
    step_x1(0)
    arrived(b_in)
    b_core = second.at[pl.ds(core * 16, 16)]
    b_in = [send(b_core, b_core, core_peer)]
    step_project(1)
    step_x2(0)
    step_x1(1)
    arrived(b_in)
    second_flat[...] = second[...].astype(F32).reshape(256, UNITS).astype(BF16)
    step_z(0)
    step_hidden(0)
    step_x2(1)
    step_xg1(0)
    step_z(1)
    step_xg2(0)
    step_hidden(1)
    step_core_g(0)
    step_xg1(1)
    step_down(0)
    step_xg2(1)
    step_core_g(1)
    step_down(1)
    own = y_sum(0)
    last_out[...] = y_sum(1).astype(BF16)
    final = send(last_out, last_in, zh_peer)
    arrived([final])
    o_ref[...] = (own + last_in[...].astype(F32)).astype(BF16)
    for copy in started:
        copy.wait_send()


SENDS = 96


def per_device(tok, gw, uw, dw, ag, bg, au, bu):
    anywhere = pl.BlockSpec(memory_space=pl.ANY)
    v = lambda *shape: pltpu.VMEM(shape, BF16)
    return pl.pallas_call(
        kernel,
        out_shape=jax.ShapeDtypeStruct((32, OUT), BF16),
        in_specs=[anywhere] * 8,
        out_specs=pl.BlockSpec(memory_space=pltpu.VMEM),
        scratch_shapes=[
            v(FEAT, UNITS), v(FEAT, UNITS), v(UNITS, OUT),
            v(4, FEAT), v(4, FEAT), v(2, UNITS), v(2, UNITS),
            v(2, 8, 32, FEAT), v(16, 8, FEAT), v(32, 8, UNITS), v(256, UNITS),
            v(2, 2, 16, 16, WIDE), v(2, 16, 16, WIDE),
            v(2, 2, 4, 16, WIDE), v(2, 2, 4, 16, WIDE),
            v(2, 2, 2, 16, WIDE), v(2, 2, 2, 16, WIDE),
            v(2, 4, 16, WIDE), v(2, 4, 16, WIDE),
            v(2, 2, 16, 8, UNITS), v(128, UNITS),
            v(2, 8, 32, OUT), v(2, 8, 32, OUT), v(32, OUT), v(32, OUT),
            pltpu.SemaphoreType.DMA((8,)),
            pltpu.SemaphoreType.DMA((SENDS,)),
            pltpu.SemaphoreType.DMA((SENDS,)),
        ],
        compiler_params=pltpu.CompilerParams(
            collective_id=0, has_side_effects=True, vmem_limit_bytes=48 * 1024 * 1024
        ),
        name="ffn",
    )(tok, gw, uw, dw, ag.T, bg, au.T, bu)


def solution(mesh):
    weight, down = P("row", "col"), P("col", "row")
    return jax.shard_map(
        per_device,
        mesh=mesh,
        in_specs=(down, weight, weight, down, weight, weight, weight, weight),
        out_specs=down,
        check_vma=False,
    )
```

time: 872 us -> 101 us (0.12)
  waiting for transfers between devices: 581 us -> 0 us
  blocking collectives: 239 us -> 0 us
  Pallas kernels: 0 us -> 92 us
  between operations: 13.8 us -> 0.02 us
  matrix products: 12.9 us -> 0 us
    unnamed x4 -> x0, waiting for transfers between devices: 305 us -> none
    all_gather x5 -> x0, blocking collectives: 239 us -> none  [the longest x1 55.4 us: per_device(): features = lax.all_gather(tokens, 'col', axis=0, tiled=True)]
    reduce_scatter x1 -> x0, waiting for transfers between devices: 214 us -> none  [per_device(): lax.psum_scatter(output_terms.astype(jnp.bfloat16), 'col', scatter_dimens...]
    pallas_call x0 -> x1, Pallas kernels: none -> 92 us  [per_device(): pl.pallas_call(kernel, out_shape=jax.ShapeDtypeStruct((32, OUT), BF16), i...]
    all_gather x1 -> x0, waiting for transfers between devices: 62.4 us -> none  [per_device(): lax.all_gather(hidden, 'row', axis=0, tiled=True)]
    dot_general x3 -> x0, matrix products: 12.9 us -> none  [the longest x1 4.78 us: per_device(): jnp.dot(features, gate_merged, preferred_element_type=jnp.float32)]
    another operation x1 -> x0, local copies, waits for them, and re-layouts: 11.1 us -> none  [per_device(): jnp.stack([gate_part, up_part], 1)]
  transfers between devices with their start and end apart: 3 -> 0, of which waited for: 3 -> 0; matrix products, arithmetic and copies ran while one was open for 0% -> 0% of each run, Pallas kernels for 0% -> 0%
where the time goes in v1:
time: 101 us; the launch traced here: 100 us
  Pallas kernels  92 us (91%)
  local copies, waits for them, and re-layouts  8.49 us (8%)
    pallas_call x1, Pallas kernels, per_device(): pl.pallas_call(kernel, out_shape=jax.ShapeDtypeStruct((32, OUT), BF16), i...  92 us
    unnamed x17, local copies, waits for them, and re-layouts  8.49 us

profile of v1, /device:TPU:1, one launch (start us, length us, event | category | flops | bytes accessed | tf_op | source)
XLA Modules:
  0.0 100.5 jit_solution(9487623098636326157)
XLA Ops:
  0.0 0.0 copy-start
  0.0 1.5 %copy-done = bf16[512,1664]{1,0:T(8,128)(2,1)S(1)} copy-done((bf16[512,1664]{1,0:T(8,128)(2,1)S(1)}, bf16[512,1664]{1,0:T(8,128)(2,1)}, u32[]{:S(2)}) %copy-start) | copy-done | bytes 1703960
  1.5 0.0 copy-start.1
  1.5 1.5 %copy-done.1 = bf16[512,1664]{1,0:T(8,128)(2,1)S(1)} copy-done((bf16[512,1664]{1,0:T(8,128)(2,1)S(1)}, bf16[512,1664]{1,0:T(8,128)(2,1)}, u32[]{:S(2)}) %copy-start.1) | copy-done | bytes 1703960
  2.9 0.0 copy-start.2
  2.9 1.5 %copy-done.2 = bf16[1664,512]{1,0:T(8,128)(2,1)S(1)} copy-done((bf16[1664,512]{1,0:T(8,128)(2,1)S(1)}, bf16[1664,512]{1,0:T(8,128)(2,1)}, u32[]{:S(2)}) %copy-start.2) | copy-done | bytes 1703960
  4.4 0.0 copy-start.3
  4.4 0.8 copy-done.3
  5.1 0.0 copy-start.4
  5.1 0.7 copy-done.4
  5.8 0.0 copy-start.5
  5.8 0.7 copy-done.5
  6.5 0.0 copy-start.6
  6.5 0.7 copy-done.6
  7.2 0.0 copy-start.7
  7.2 0.7 copy-done.7
  7.9 92.0 %ffn.1 = bf16[32,512]{1,0:T(8,128)(2,1)S(1)} custom-call(bf16[32,512]{1,0:T(8,128)(2,1)S(1)} %copy-done.3, bf16[512,1664]{1,0:T(8,128)(2,1)S(1)} %copy-done, bf16[512,1664]{1,0:T(8,128)(2,1)S(1)} %copy-done.1, bf16[1664,512]{1,0:T(8,128)(2,1)S(1)} %copy-done.2, bf16[4,512]{1,0:T(4,128)(2,1)S(1)} %bitcast.2, bf16[2,1664]{1,0:T(2,128)(2,1)S(1)} %copy-done.4, ...), custom_call_target="tpu_custom_call" | custom-call | tf_op jit(solution)/shard_map/ffn/pallas_call | solution.py:329
  99.9 0.6 copy.10
Async XLA Ops:
  0.0 1.5 %copy-start = (bf16[512,1664]{1,0:T(8,128)(2,1)S(1)}, bf16[512,1664]{1,0:T(8,128)(2,1)}, u32[]{:S(2)}) copy-start(bf16[512,1664]{1,0:T(8,128)(2,1)} %gw_hbm.1) | copy-start | bytes 5111812
  1.5 1.5 %copy-start.1 = (bf16[512,1664]{1,0:T(8,128)(2,1)S(1)}, bf16[512,1664]{1,0:T(8,128)(2,1)}, u32[]{:S(2)}) copy-start(bf16[512,1664]{1,0:T(8,128)(2,1)} %uw_hbm.1) | copy-start | bytes 5111812
  2.9 1.5 %copy-start.2 = (bf16[1664,512]{1,0:T(8,128)(2,1)S(1)}, bf16[1664,512]{1,0:T(8,128)(2,1)}, u32[]{:S(2)}) copy-start(bf16[1664,512]{1,0:T(8,128)(2,1)} %dw_hbm.1) | copy-start | bytes 5111812
  4.4 0.8 copy-start.3
  5.1 0.7 copy-start.4
  5.8 0.7 copy-start.5
  6.5 0.7 copy-start.6
  7.2 0.7 copy-start.7

commit v2 on v0

v2 whole, which is shorter than its diff:
```python
import jax
import jax.numpy as jnp
from jax import lax
from jax.experimental import pallas as pl
from jax.experimental.pallas import tpu as pltpu
from jax.sharding import PartitionSpec as P

FEAT = 512
UNITS = 1664
RANKS = 128
PART = 896
PARTS = (896, 768)
OUT = 512
MESH = pl.DeviceIdType.MESH
F32 = jnp.float32
BF16 = jnp.bfloat16


def kernel(
    tok_hbm, gw_hbm, uw_hbm, dw_hbm, ag_hbm, bg_hbm, au_hbm, bu_hbm,
    o_ref,
    gw, uw, dw, ag, au, bg, bu,
    tok, first, first_flat, second, second_flat, rank_sums,
    part, from_core, x1_out, x1_in, x2_out, x2_in, z_out, z_in,
    hid, hid_flat, out_terms, y1_in, y2_out, y2_in, y3_in, y4_in, last_out, last_in,
    local_sem, send_sem, recv_sem,
):
    row, col = lax.axis_index("row"), lax.axis_index("col")
    x, z, core = row // 8, (row // 2) % 4, row % 2
    y, zh = col // 2, col % 2

    def device(x=x, z=z, core=core, y=y, zh=zh):
        return ((x * 4 + z) * 2 + core, y * 2 + zh)

    other = 1 - core
    ring_a = device(x=x + 1 - 2 * (x % 2))
    ring_b = device(x=3 - x)
    bit_b = x // 2
    bit_a = (x % 2 + bit_b) % 2
    far_x = device(x=(x + 2) % 4)
    core_peer = device(core=other)
    zh_peer = device(zh=1 - zh)
    y_peer = {k: device(y=(y + k) % 8) for k in (1, -1, 2, -2, 3, -3, 4)}
    z_peers = [device(z=(z + k) % 4) for k in range(1, 4)]

    def fetch(src, dst, n):
        copy = pltpu.make_async_copy(src, dst, local_sem.at[n])
        copy.start()
        return copy

    barrier = pltpu.get_barrier_semaphore()
    partners = [zh_peer, *y_peer.values(), *z_peers, ring_a, ring_b, far_x, core_peer]
    for peer in partners:
        pl.semaphore_signal(barrier, inc=1, device_id=peer, device_id_type=MESH)

    small = [
        fetch(ag_hbm, ag, 0), fetch(au_hbm, au, 1), fetch(bg_hbm, bg, 2), fetch(bu_hbm, bu, 3),
    ]
    own_tokens = fetch(tok_hbm, tok.at[zh, y], 4)
    weights = [fetch(gw_hbm, gw, 5), fetch(uw_hbm, uw, 6)]
    down = fetch(dw_hbm, dw, 7)

    for copy in small:
        copy.wait()
    a_g, a_u = ag[...].astype(F32), au[...].astype(F32)
    first[col] = jnp.concatenate([a_g[0:2], a_u[0:2], a_g[2:4], a_u[2:4]], 0).astype(BF16)
    b_rows = jnp.concatenate([bg[...].astype(F32), bu[...].astype(F32)], 0)
    b_tail = jnp.concatenate([b_rows[:, PART:], jnp.zeros((4, 2 * PART - UNITS), F32)], 1)
    slot_b = core * 16 + x * 4 + z
    second[slot_b] = jnp.concatenate([b_rows[:, :PART], b_tail], 0).astype(BF16)
    pl.semaphore_wait(barrier, len(partners))

    started = []

    def send(src, dst, peer):
        n = len(started)
        copy = pltpu.make_async_remote_copy(
            src_ref=src, dst_ref=dst, send_sem=send_sem.at[n], recv_sem=recv_sem.at[n],
            device_id=peer, device_id_type=MESH,
        )
        copy.start()
        started.append(copy)
        return copy

    def arrived(copies):
        for copy in copies:
            copy.wait_recv()

    def block(side, at):
        return tok.at[side, (y + at) % 8]

    def spread_tokens(side, src):
        return [send(src, block(side, 0), y_peer[k]) for k in (2, -2, 1, -1)]

    def relay_tokens(side, copies):
        arrived(copies[:2])
        low, high = pl.ds(0, 16), pl.ds(16, 16)
        below, above = block(side, -2), block(side, 2)
        return copies[2:] + [
            send(below.at[low], below.at[low], y_peer[2]),
            send(above.at[high], above.at[high], y_peer[-2]),
            send(below, below, y_peer[1]),
            send(above, above, y_peer[-1]),
        ]

    def spread_first(side):
        ref = first.at[y * 2 + side]
        return [send(ref, ref, y_peer[k]) for k in (4, 3, -3, 2, -2, 1, -1)]

    a_zh = [send(first.at[col], first.at[col], zh_peer)]
    tok_zh = [send(tok_hbm, block(zh, 0), zh_peer)]
    tok_in = [spread_tokens(zh, tok_hbm), None]
    a_in = spread_first(zh)
    b_in = [send(second.at[slot_b], second.at[slot_b], peer) for peer in z_peers]

    gate_lane = lax.broadcasted_iota(jnp.int32, (128, RANKS), 1) % 4 < 2

    def project(q, c, half):
        side = zh if q == 0 else 1 - zh
        x_blk = tok[side, pl.ds(half * 4, 4)].reshape(128, FEAT)

        def paired(g, u):
            pair = jnp.stack([g.reshape(16, 8, 128), u.reshape(16, 8, 128)], 1)
            return pair.reshape(16, 16, 128).astype(BF16)

        for at in range(0, PARTS[c], 128):
            w_at = c * PART + at
            w = jnp.concatenate([gw[:, w_at : w_at + 128], uw[:, w_at : w_at + 128]], 1)
            both = jnp.dot(x_blk, w, preferred_element_type=F32)
            part[q, c, half, :, :, at : at + 128] = paired(both[:, :128], both[:, 128:])
        if c == 1:
            ranks = lax.dot_general(
                x_blk, first_flat[...], (((1,), (1,)), ((), ())), preferred_element_type=F32
            )
            part[q, c, half, :, :, PARTS[1] : PART] = paired(
                jnp.where(gate_lane, ranks, 0.0), jnp.where(gate_lane, 0.0, ranks)
            )

    split = ((bit_a, bit_b), (bit_b, bit_a))
    first_peer, second_peer = (ring_a, ring_b), (ring_b, ring_a)
    core_in, x1, x2, z_arr, zg, xg1, xg2, core_g = ({} for _ in range(8))

    def step_project(q, c):
        project(q, c, other)
        core_in[q, c] = send(part.at[q, c, other], from_core.at[q, c], core_peer)
        project(q, c, core)

    def step_x1(q, c):
        arrived([core_in[q, c]])
        x1[q, c] = []
        for h in (0, 1):
            base = h * 8 + (1 - split[h][0]) * 4
            for i in range(4):
                total = part[q, c, core, base + i].astype(F32)
                total = total + from_core[q, c, base + i].astype(F32)
                x1_out[q, c, h, i] = total.astype(BF16)
            x1[q, c].append(send(x1_out.at[q, c, h], x1_in.at[q, c, h], first_peer[h]))

    def step_x2(q, c):
        x2[q, c] = []
        for h in (0, 1):
            arrived(x1[q, c][h : h + 1])
            s = 1 - split[h][1]
            base = h * 8 + split[h][0] * 4 + s * 2
            for i in range(2):
                total = part[q, c, core, base + i].astype(F32)
                total = total + from_core[q, c, base + i].astype(F32)
                total = total + x1_in[q, c, h, s * 2 + i].astype(F32)
                x2_out[q, c, h, i] = total.astype(BF16)
            x2[q, c].append(send(x2_out.at[q, c, h], x2_in.at[q, c, h], second_peer[h]))

    def slot_of(k):
        h, low = k // 2, k % 2
        p = jnp.where(h == 0, bit_a, bit_b)
        s = jnp.where(h == 0, bit_b, bit_a)
        return h, s, low, h * 8 + p * 4 + s * 2 + low

    def kept_terms(q, c, k):
        h, s, low, at = slot_of(k)
        return (
            part[q, c, core, at].astype(F32)
            + from_core[q, c, at].astype(F32)
            + x1_in[q, c, h, s * 2 + low].astype(F32)
            + x2_in[q, c, h, low].astype(F32)
        )

    def step_z(q, c):
        arrived(x2[q, c])
        z_arr[q, c] = []
        for k in (2, 1, 3):
            z_out[q, c, k] = kept_terms(q, c, (z + k) % 4).astype(BF16)
            z_arr[q, c].append(send(z_out.at[q, c, k], z_in.at[q, c, k], z_peers[k - 1]))

    def step_hidden(q, c):
        total = kept_terms(q, c, z)
        arrived(z_arr[q, c])
        for k in range(1, 4):
            total = total + z_in[q, c, k].astype(F32)
        if c == 1:
            k_at = lax.broadcasted_iota(jnp.int32, (RANKS, 256), 0)
            s_at = lax.broadcasted_iota(jnp.int32, (RANKS, 256), 1)
            r_of = k_at // 4
            meets = ((r_of % 2) * 16 + r_of // 2) * 8 + k_at % 4
            ranks = total[:, PARTS[1] :].astype(BF16)
            for n in (0, 1):
                spread = jnp.where(meets + n * 4 == s_at, 2.0, 0.0).astype(BF16)
                rank_sums[q, n] = jnp.dot(
                    ranks, spread, preferred_element_type=F32
                ).astype(BF16)
        both = total[:, : PARTS[c]] + jnp.dot(
            rank_sums[q, c], second_flat[:, : PARTS[c]], preferred_element_type=F32
        )
        gate, up = both[:8], both[8:]
        at = slot_of(z)[3]
        hid[q, c, core, at, :, : PARTS[c]] = (gate / (1.0 + jnp.exp(-gate)) * up).astype(BF16)
        zg[q, c] = [send_hidden(q, c, at, 1, z_peers[k - 1]) for k in (2, 1, 3)]

    def send_hidden(q, c, at, n, peer):
        ref = hid.at[q, c, core, pl.ds(at, n), :, pl.ds(0, PARTS[c])]
        return send(ref, ref, peer)

    def step_xg1(q, c):
        arrived(zg[q, c])
        xg1[q, c] = [
            send_hidden(q, c, h * 8 + split[h][0] * 4 + split[h][1] * 2, 2, second_peer[h])
            for h in (0, 1)
        ]

    def step_xg2(q, c):
        xg2[q, c] = []
        for h in (0, 1):
            arrived(xg1[q, c][h : h + 1])
            xg2[q, c].append(send_hidden(q, c, h * 8 + split[h][0] * 4, 4, first_peer[h]))

    def step_core_g(q, c):
        arrived(xg2[q, c])
        core_g[q, c] = send_hidden(q, c, 0, 16, core_peer)

    def down_half(q, half):
        for c in (0, 1):
            for i in range(0, 16, 2):
                two = hid[q, c, half, i : i + 2, :, : PARTS[c]].astype(F32)
                hid_flat[i * 8 : i * 8 + 16, c * PART : c * PART + PARTS[c]] = two.reshape(
                    16, PARTS[c]
                ).astype(BF16)
        for at in (0, 256):
            terms = jnp.dot(hid_flat[...], dw[:, at : at + 256], preferred_element_type=F32)
            out_terms[q, pl.ds(half * 4, 4), :, at : at + 256] = terms.astype(BF16).reshape(
                4, 32, 256
            )

    y1, y2, y34 = {}, {}, {}

    def step_down(q):
        if q == 0:
            down.wait()
        down_half(q, core)
        arrived([core_g[q, 0], core_g[q, 1]])
        down_half(q, other)

        def terms(k):
            return out_terms.at[q, (y + k) % 8]

        low, high = pl.ds(0, 16), pl.ds(16, 16)
        y34[q] = [
            send(terms(4).at[low], y4_in.at[q, 0], y_peer[2]),
            send(terms(4).at[high], y4_in.at[q, 1], y_peer[-2]),
            send(terms(3), y3_in.at[q, 0], y_peer[1]),
            send(terms(-3), y3_in.at[q, 1], y_peer[-1]),
        ]
        y1[q] = [
            send(terms(1), y1_in.at[q, 0], y_peer[1]),
            send(terms(-1), y1_in.at[q, 1], y_peer[-1]),
        ]

    def step_y2(q):
        arrived(y34[q])
        y2[q] = []
        for n, k in ((0, 2), (1, -2)):
            total = out_terms[q, (y + k) % 8].astype(F32) + y3_in[q, n].astype(F32)
            mine, rest = (total[:16], total[16:]) if n == 0 else (total[16:], total[:16])
            mine = mine + y4_in[q, n].astype(F32)
            y2_out[q, n] = jnp.concatenate(
                [mine, rest] if n == 0 else [rest, mine], 0
            ).astype(BF16)
            y2[q].append(send(y2_out.at[q, n], y2_in.at[q, n], y_peer[k]))

    def y_sum(q):
        arrived(y1[q])
        total = out_terms[q, y].astype(F32)
        total = total + y1_in[q, 0].astype(F32) + y1_in[q, 1].astype(F32)
        arrived(y2[q])
        return total + y2_in[q, 0].astype(F32) + y2_in[q, 1].astype(F32)

    tok_in[0] = relay_tokens(zh, tok_in[0])
    arrived(a_zh)
    a_in = a_in + spread_first(1 - zh)
    arrived(tok_zh)
    tok_in[1] = spread_tokens(1 - zh, block(1 - zh, 0))
    arrived(b_in)
    b_x = second.at[pl.ds(core * 16 + x * 4, 4)]
    b_in = [send(b_x, b_x, peer) for peer in (far_x, ring_a, ring_b)]
    own_tokens.wait()
    weights[0].wait()
    weights[1].wait()
    arrived(tok_in[0])
    step_project(0, 0)
    arrived(a_in)
    first_flat[...] = first[...].astype(F32).reshape(RANKS, FEAT).astype(BF16)
    step_project(0, 1)
    step_x1(0, 0)
    tok_in[1] = relay_tokens(1 - zh, tok_in[1])
    step_x1(0, 1)
    arrived(b_in)
    b_core = second.at[pl.ds(core * 16, 16)]
    b_in = [send(b_core, b_core, core_peer)]
    arrived(tok_in[1])
    step_project(1, 1)
    step_project(1, 0)
    step_x2(0, 0)
    step_x1(1, 1)
    step_x2(0, 1)
    step_x1(1, 0)
    step_z(0, 0)
    arrived(b_in)
    second_flat[...] = second[...].astype(F32).reshape(256, PART).astype(BF16)
    step_x2(1, 1)
    step_z(0, 1)
    step_x2(1, 0)
    step_hidden(0, 1)
    step_hidden(0, 0)
    step_z(1, 1)
    step_xg1(0, 1)
    step_z(1, 0)
    step_xg1(0, 0)
    step_hidden(1, 1)
    step_xg2(0, 1)
    step_hidden(1, 0)
    step_xg2(0, 0)
    step_xg1(1, 1)
    step_core_g(0, 1)
    step_xg1(1, 0)
    step_core_g(0, 0)
    step_xg2(1, 1)
    step_xg2(1, 0)
    step_down(0)
    step_core_g(1, 1)
    step_core_g(1, 0)
    step_y2(0)
    step_down(1)
    own = y_sum(0)
    step_y2(1)
    last_out[...] = y_sum(1).astype(BF16)
    final = send(last_out, last_in, zh_peer)
    arrived([final])
    o_ref[...] = (own + last_in[...].astype(F32)).astype(BF16)
    for copy in started:
        copy.wait_send()


SENDS = 144


def per_device(tok, gw, uw, dw, ag, bg, au, bu):
    in_hbm = pl.BlockSpec(memory_space=pltpu.HBM)
    v = lambda *shape: pltpu.VMEM(shape, BF16)
    return pl.pallas_call(
        kernel,
        out_shape=jax.ShapeDtypeStruct((32, OUT), BF16),
        in_specs=[in_hbm] * 8,
        out_specs=pl.BlockSpec(memory_space=pltpu.VMEM),
        scratch_shapes=[
            v(FEAT, UNITS), v(FEAT, UNITS), v(UNITS, OUT),
            v(4, FEAT), v(4, FEAT), v(2, UNITS), v(2, UNITS),
            v(2, 8, 32, FEAT), v(16, 8, FEAT), v(RANKS, FEAT),
            v(32, 8, PART), v(256, PART), v(2, 2, 16, 256),
            v(2, 2, 2, 16, 16, PART), v(2, 2, 16, 16, PART),
            v(2, 2, 2, 4, 16, PART), v(2, 2, 2, 4, 16, PART),
            v(2, 2, 2, 2, 16, PART), v(2, 2, 2, 2, 16, PART),
            v(2, 2, 4, 16, PART), v(2, 2, 4, 16, PART),
            v(2, 2, 2, 16, 8, PART), v(128, UNITS),
            v(2, 8, 32, OUT), v(2, 2, 32, OUT), v(2, 2, 32, OUT), v(2, 2, 32, OUT),
            v(2, 2, 32, OUT), v(2, 2, 16, OUT), v(32, OUT), v(32, OUT),
            pltpu.SemaphoreType.DMA((8,)),
            pltpu.SemaphoreType.DMA((SENDS,)),
            pltpu.SemaphoreType.DMA((SENDS,)),
        ],
        compiler_params=pltpu.CompilerParams(
            collective_id=0, has_side_effects=True, vmem_limit_bytes=60 * 1024 * 1024
        ),
        name="ffn",
    )(tok, gw, uw, dw, ag.T, bg, au.T, bu)


def solution(mesh):
    weight, down = P("row", "col"), P("col", "row")
    return jax.shard_map(
        per_device,
        mesh=mesh,
        in_specs=(down, weight, weight, down, weight, weight, weight, weight),
        out_specs=down,
        check_vma=False,
    )
```

time: 872 us -> 84 us (0.10)
  waiting for transfers between devices: 581 us -> 0 us
  blocking collectives: 239 us -> 0 us
  Pallas kernels: 0 us -> 81.8 us
  between operations: 13.8 us -> 0.01 us
  matrix products: 12.9 us -> 0 us
  local copies, waits for them, and re-layouts: 13.8 us -> 1.38 us
    unnamed x4 -> x0, waiting for transfers between devices: 305 us -> none
    all_gather x5 -> x0, blocking collectives: 239 us -> none  [the longest x1 55.4 us: per_device(): features = lax.all_gather(tokens, 'col', axis=0, tiled=True)]
    reduce_scatter x1 -> x0, waiting for transfers between devices: 214 us -> none  [per_device(): lax.psum_scatter(output_terms.astype(jnp.bfloat16), 'col', scatter_dimens...]
    pallas_call x0 -> x1, Pallas kernels: none -> 81.8 us  [per_device(): pl.pallas_call(kernel, out_shape=jax.ShapeDtypeStruct((32, OUT), BF16), i...]
    all_gather x1 -> x0, waiting for transfers between devices: 62.4 us -> none  [per_device(): lax.all_gather(hidden, 'row', axis=0, tiled=True)]
    dot_general x3 -> x0, matrix products: 12.9 us -> none  [the longest x1 4.78 us: per_device(): jnp.dot(features, gate_merged, preferred_element_type=jnp.float32)]
    another operation x1 -> x0, local copies, waits for them, and re-layouts: 11.1 us -> none  [per_device(): jnp.stack([gate_part, up_part], 1)]
  transfers between devices with their start and end apart: 3 -> 0, of which waited for: 3 -> 0; matrix products, arithmetic and copies ran while one was open for 0% -> 0% of each run, Pallas kernels for 0% -> 0%
where the time goes in v2:
time: 84 us; the launch traced here: 83.2 us
  Pallas kernels  81.8 us (97%)
  local copies, waits for them, and re-layouts  1.38 us (2%)
    pallas_call x1, Pallas kernels, per_device(): pl.pallas_call(kernel, out_shape=jax.ShapeDtypeStruct((32, OUT), BF16), i...  81.8 us

profile of v2, /device:TPU:1, one launch (start us, length us, event | category | flops | bytes accessed | tf_op | source)
XLA Modules:
  0.0 83.2 jit_solution(12333848529979892656)
XLA Ops:
  0.0 81.8 %ffn.1 = bf16[32,512]{1,0:T(8,128)(2,1)} custom-call(bf16[32,512]{1,0:T(8,128)(2,1)} %tok_hbm.1, bf16[512,1664]{1,0:T(8,128)(2,1)} %gw_hbm.1, bf16[512,1664]{1,0:T(8,128)(2,1)} %uw_hbm.1, bf16[1664,512]{1,0:T(8,128)(2,1)} %dw_hbm.1, bf16[4,512]{1,0:T(4,128)(2,1)} %bitcast.2, bf16[2,1664]{1,0:T(2,128)(2,1)} %bg_hbm.1, bf16[4,512]{1,0:T(4,128)(2,1)} %bitcast.3, ...), custom_call_target="tpu_custom_call" | custom-call | tf_op jit(solution)/shard_map/ffn/pallas_call | solution.py:367
  81.8 1.4 %copy.10 = bf16[32,512]{1,0:T(8,128)(2,1)} copy(bf16[32,512]{1,0:T(8,128)(2,1)} %ffn.1) | data formatting | bytes 65536

commit v3 on v2

--- a/solution.py
+++ b/solution.py
@@ -57,9 +57,6 @@
         fetch(ag_hbm, ag, 0), fetch(au_hbm, au, 1), fetch(bg_hbm, bg, 2), fetch(bu_hbm, bu, 3),
     ]
     own_tokens = fetch(tok_hbm, tok.at[zh, y], 4)
-    weights = [fetch(gw_hbm, gw, 5), fetch(uw_hbm, uw, 6)]
-    down = fetch(dw_hbm, dw, 7)
-
     for copy in small:
         copy.wait()
     a_g, a_u = ag[...].astype(F32), au[...].astype(F32)
@@ -72,19 +69,54 @@
 
     started = []
 
-    def send(src, dst, peer):
+    def send(src, dst, peer, start=True):
         n = len(started)
         copy = pltpu.make_async_remote_copy(
             src_ref=src, dst_ref=dst, send_sem=send_sem.at[n], recv_sem=recv_sem.at[n],
             device_id=peer, device_id_type=MESH,
         )
-        copy.start()
+        if start:
+            copy.start()
         started.append(copy)
         return copy
 
     def arrived(copies):
         for copy in copies:
             copy.wait_recv()
+
+    def send_each(n, refs, before=None):
+        first_sem = len(started)
+
+        def make(i):
+            src, dst, peer = refs(i)
+            return pltpu.make_async_remote_copy(
+                src_ref=src, dst_ref=dst, send_sem=send_sem.at[first_sem + i],
+                recv_sem=recv_sem.at[first_sem + i], device_id=peer, device_id_type=MESH,
+            )
+
+        def go(i, carry):
+            if before is not None:
+                before(i)
+            make(i).start()
+            return carry
+
+        lax.fori_loop(0, n, go, 0)
+        started.extend(make(i) for i in range(n))
+
+        def wait_one(i, carry):
+            make(i).wait_recv()
+            return carry
+
+        def wait_all():
+            lax.fori_loop(0, n, wait_one, 0)
+
+        wait_all.one = lambda i: make(i).wait_recv()
+        return wait_all
+
+    def pick(h, a, b):
+        if isinstance(h, int):
+            return b if h else a
+        return jnp.where(h == 0, a, b)
 
     def block(side, at):
         return tok.at[side, (y + at) % 8]
@@ -105,13 +137,17 @@
 
     def spread_first(side):
         ref = first.at[y * 2 + side]
-        return [send(ref, ref, y_peer[k]) for k in (4, 3, -3, 2, -2, 1, -1)]
+        return send_each(7, lambda i: (ref, ref, device(y=(y + 1 + i) % 8)))
 
     a_zh = [send(first.at[col], first.at[col], zh_peer)]
     tok_zh = [send(tok_hbm, block(zh, 0), zh_peer)]
     tok_in = [spread_tokens(zh, tok_hbm), None]
-    a_in = spread_first(zh)
-    b_in = [send(second.at[slot_b], second.at[slot_b], peer) for peer in z_peers]
+    a_own_in = spread_first(zh)
+    b_own = second.at[slot_b]
+    b_in = send_each(3, lambda i: (b_own, b_own, device(z=(z + 1 + i) % 4)))
+
+    weights = [fetch(gw_hbm, gw, 5), fetch(uw_hbm, uw, 6)]
+    down = fetch(dw_hbm, dw, 7)
 
     gate_lane = lax.broadcasted_iota(jnp.int32, (128, RANKS), 1) % 4 < 2
 
@@ -136,38 +172,63 @@
                 jnp.where(gate_lane, ranks, 0.0), jnp.where(gate_lane, 0.0, ranks)
             )
 
-    split = ((bit_a, bit_b), (bit_b, bit_a))
-    first_peer, second_peer = (ring_a, ring_b), (ring_b, ring_a)
-    core_in, x1, x2, z_arr, zg, xg1, xg2, core_g = ({} for _ in range(8))
+    x_a, x_b = x + 1 - 2 * (x % 2), 3 - x
+
+    def ring(h):
+        return device(x=pick(h, x_a, x_b))
+
+    core_in, x1, x2, z_arr, zg, xg, core_g = ({} for _ in range(7))
 
     def step_project(q, c):
-        project(q, c, other)
-        core_in[q, c] = send(part.at[q, c, other], from_core.at[q, c], core_peer)
-        project(q, c, core)
+        core_in[q, c] = send(part.at[q, c, other], from_core.at[q, c], core_peer, start=False)
+
+        def half_step(n, carry):
+            project(q, c, pick(n, other, core))
+
+            @pl.when(n == 0)
+            def _():
+                core_in[q, c].start()
+
+            return carry
+
+        lax.fori_loop(0, 2, half_step, 0)
 
     def step_x1(q, c):
         arrived([core_in[q, c]])
-        x1[q, c] = []
-        for h in (0, 1):
-            base = h * 8 + (1 - split[h][0]) * 4
-            for i in range(4):
+
+        def sums(h):
+            base = h * 8 + (1 - pick(h, bit_a, bit_b)) * 4
+
+            def group(i, carry):
                 total = part[q, c, core, base + i].astype(F32)
                 total = total + from_core[q, c, base + i].astype(F32)
                 x1_out[q, c, h, i] = total.astype(BF16)
-            x1[q, c].append(send(x1_out.at[q, c, h], x1_in.at[q, c, h], first_peer[h]))
+                return carry
+
+            lax.fori_loop(0, 4, group, 0, unroll=2)
+
+        x1[q, c] = send_each(
+            2,
+            lambda h: (x1_out.at[q, c, h], x1_in.at[q, c, h], ring(h)),
+            sums,
+        )
 
     def step_x2(q, c):
-        x2[q, c] = []
-        for h in (0, 1):
-            arrived(x1[q, c][h : h + 1])
-            s = 1 - split[h][1]
-            base = h * 8 + split[h][0] * 4 + s * 2
+        def sums(h):
+            x1[q, c].one(h)
+            s = 1 - pick(h, bit_b, bit_a)
+            base = h * 8 + pick(h, bit_a, bit_b) * 4 + s * 2
             for i in range(2):
                 total = part[q, c, core, base + i].astype(F32)
                 total = total + from_core[q, c, base + i].astype(F32)
                 total = total + x1_in[q, c, h, s * 2 + i].astype(F32)
                 x2_out[q, c, h, i] = total.astype(BF16)
-            x2[q, c].append(send(x2_out.at[q, c, h], x2_in.at[q, c, h], second_peer[h]))
+
+        x2[q, c] = send_each(
+            2,
+            lambda h: (x2_out.at[q, c, h], x2_in.at[q, c, h], ring(1 - h)),
+            sums,
+        )
 
     def slot_of(k):
         h, low = k // 2, k % 2
@@ -185,16 +246,21 @@
         )
 
     def step_z(q, c):
-        arrived(x2[q, c])
-        z_arr[q, c] = []
-        for k in (2, 1, 3):
-            z_out[q, c, k] = kept_terms(q, c, (z + k) % 4).astype(BF16)
-            z_arr[q, c].append(send(z_out.at[q, c, k], z_in.at[q, c, k], z_peers[k - 1]))
+        x2[q, c]()
+
+        def sums(i):
+            z_out[q, c, i] = kept_terms(q, c, (z + 1 + i) % 4).astype(BF16)
+
+        z_arr[q, c] = send_each(
+            3,
+            lambda i: (z_out.at[q, c, i], z_in.at[q, c, i], device(z=(z + 1 + i) % 4)),
+            sums,
+        )
 
     def step_hidden(q, c):
         total = kept_terms(q, c, z)
-        arrived(z_arr[q, c])
-        for k in range(1, 4):
+        z_arr[q, c]()
+        for k in range(3):
             total = total + z_in[q, c, k].astype(F32)
         if c == 1:
             k_at = lax.broadcasted_iota(jnp.int32, (RANKS, 256), 0)
@@ -211,36 +277,36 @@
             rank_sums[q, c], second_flat[:, : PARTS[c]], preferred_element_type=F32
         )
         gate, up = both[:8], both[8:]
-        at = slot_of(z)[3]
+        at = x * 4 + z
         hid[q, c, core, at, :, : PARTS[c]] = (gate / (1.0 + jnp.exp(-gate)) * up).astype(BF16)
-        zg[q, c] = [send_hidden(q, c, at, 1, z_peers[k - 1]) for k in (2, 1, 3)]
-
-    def send_hidden(q, c, at, n, peer):
-        ref = hid.at[q, c, core, pl.ds(at, n), :, pl.ds(0, PARTS[c])]
-        return send(ref, ref, peer)
-
-    def step_xg1(q, c):
-        arrived(zg[q, c])
-        xg1[q, c] = [
-            send_hidden(q, c, h * 8 + split[h][0] * 4 + split[h][1] * 2, 2, second_peer[h])
-            for h in (0, 1)
-        ]
-
-    def step_xg2(q, c):
-        xg2[q, c] = []
-        for h in (0, 1):
-            arrived(xg1[q, c][h : h + 1])
-            xg2[q, c].append(send_hidden(q, c, h * 8 + split[h][0] * 4, 4, first_peer[h]))
+        zg[q, c] = send_hidden(q, c, 3, lambda i: at, 1, lambda i: device(z=(z + 1 + i) % 4))
+
+    def send_hidden(q, c, n, at, groups, peer):
+        def refs(i):
+            ref = hid.at[q, c, core, pl.ds(at(i), groups), :, pl.ds(0, PARTS[c])]
+            return ref, ref, peer(i)
+
+        return send_each(n, refs)
+
+    def step_xg(q, c):
+        zg[q, c]()
+        xg[q, c] = send_hidden(
+            q, c, 3, lambda i: x * 4, 4, lambda i: device(x=(x + 1 + i) % 4)
+        )
 
     def step_core_g(q, c):
-        arrived(xg2[q, c])
-        core_g[q, c] = send_hidden(q, c, 0, 16, core_peer)
+        xg[q, c]()
+        ref = hid.at[q, c, core, :, :, pl.ds(0, PARTS[c])]
+        core_g[q, c] = send(ref, ref, core_peer)
 
     def down_half(q, half):
         for c in (0, 1):
-            for i in range(0, 16, 2):
-                two = hid[q, c, half, i : i + 2, :, : PARTS[c]].astype(F32)
-                hid_flat[i * 8 : i * 8 + 16, c * PART : c * PART + PARTS[c]] = two.reshape(
+            for i in range(8):
+                h, p, s = i // 4, i // 2 % 2, i % 2
+                on_a, on_b = (p, s) if h == 0 else (s, p)
+                slot = (2 * on_b + (on_a + on_b) % 2) * 4 + h * 2
+                two = hid[q, c, half, slot : slot + 2, :, : PARTS[c]].astype(F32)
+                hid_flat[i * 16 : i * 16 + 16, c * PART : c * PART + PARTS[c]] = two.reshape(
                     16, PARTS[c]
                 ).astype(BF16)
         for at in (0, 256):
@@ -294,24 +360,25 @@
 
     tok_in[0] = relay_tokens(zh, tok_in[0])
     arrived(a_zh)
-    a_in = a_in + spread_first(1 - zh)
+    a_other_in = spread_first(1 - zh)
     arrived(tok_zh)
     tok_in[1] = spread_tokens(1 - zh, block(1 - zh, 0))
-    arrived(b_in)
+    b_in()
     b_x = second.at[pl.ds(core * 16 + x * 4, 4)]
-    b_in = [send(b_x, b_x, peer) for peer in (far_x, ring_a, ring_b)]
+    b_in = send_each(3, lambda i: (b_x, b_x, device(x=(x + 1 + i) % 4)))
     own_tokens.wait()
     weights[0].wait()
     weights[1].wait()
     arrived(tok_in[0])
     step_project(0, 0)
-    arrived(a_in)
+    a_own_in()
+    a_other_in()
     first_flat[...] = first[...].astype(F32).reshape(RANKS, FEAT).astype(BF16)
     step_project(0, 1)
     step_x1(0, 0)
     tok_in[1] = relay_tokens(1 - zh, tok_in[1])
     step_x1(0, 1)
-    arrived(b_in)
+    b_in()
     b_core = second.at[pl.ds(core * 16, 16)]
     b_in = [send(b_core, b_core, core_peer)]
     arrived(tok_in[1])
@@ -330,19 +397,15 @@
     step_hidden(0, 1)
     step_hidden(0, 0)
     step_z(1, 1)
-    step_xg1(0, 1)
+    step_xg(0, 1)
     step_z(1, 0)
-    step_xg1(0, 0)
+    step_xg(0, 0)
     step_hidden(1, 1)
-    step_xg2(0, 1)
+    step_core_g(0, 1)
     step_hidden(1, 0)
-    step_xg2(0, 0)
-    step_xg1(1, 1)
-    step_core_g(0, 1)
-    step_xg1(1, 0)
     step_core_g(0, 0)
-    step_xg2(1, 1)
-    step_xg2(1, 0)
+    step_xg(1, 1)
+    step_xg(1, 0)
     step_down(0)
     step_core_g(1, 1)
     step_core_g(1, 0)
@@ -386,7 +449,7 @@
             pltpu.SemaphoreType.DMA((SENDS,)),
         ],
         compiler_params=pltpu.CompilerParams(
-            collective_id=0, has_side_effects=True, vmem_limit_bytes=60 * 1024 * 1024
+            collective_id=0, has_side_effects=True, vmem_limit_bytes=56 * 1024 * 1024
         ),
         name="ffn",
     )(tok, gw, uw, dw, ag.T, bg, au.T, bu)

time: 84 us -> 81.5 us (0.970)
  Pallas kernels: 81.8 us -> 79 us
    pallas_call x1, Pallas kernels: 81.8 us -> 79 us  [per_device(): pl.pallas_call(kernel, out_shape=jax.ShapeDtypeStruct((32, OUT), BF16), i...]
where the time goes in v3:
time: 81.5 us; the launch traced here: 80.4 us
  Pallas kernels  79 us (97%)
  local copies, waits for them, and re-layouts  1.38 us (2%)
    pallas_call x1, Pallas kernels, per_device(): pl.pallas_call(kernel, out_shape=jax.ShapeDtypeStruct((32, OUT), BF16), i...  79 us

profile of v3, /device:TPU:1, one launch (start us, length us, event | category | flops | bytes accessed | tf_op | source)
XLA Modules:
  0.0 80.4 jit_solution(13243542664654364432)
XLA Ops:
  0.0 79.0 %ffn.1 = bf16[32,512]{1,0:T(8,128)(2,1)} custom-call(bf16[32,512]{1,0:T(8,128)(2,1)} %tok_hbm.1, bf16[512,1664]{1,0:T(8,128)(2,1)} %gw_hbm.1, bf16[512,1664]{1,0:T(8,128)(2,1)} %uw_hbm.1, bf16[1664,512]{1,0:T(8,128)(2,1)} %dw_hbm.1, bf16[4,512]{1,0:T(4,128)(2,1)} %bitcast.2, bf16[2,1664]{1,0:T(2,128)(2,1)} %bg_hbm.1, bf16[4,512]{1,0:T(4,128)(2,1)} %bitcast.3, ...), custom_call_target="tpu_custom_call" | custom-call | tf_op jit(solution)/shard_map/ffn/pallas_call | solution.py:430
  79.0 1.4 %copy.10 = bf16[32,512]{1,0:T(8,128)(2,1)} copy(bf16[32,512]{1,0:T(8,128)(2,1)} %ffn.1) | data formatting | bytes 65536

commit v4 on v3

--- a/solution.py
+++ b/solution.py
@@ -57,14 +57,6 @@
         fetch(ag_hbm, ag, 0), fetch(au_hbm, au, 1), fetch(bg_hbm, bg, 2), fetch(bu_hbm, bu, 3),
     ]
     own_tokens = fetch(tok_hbm, tok.at[zh, y], 4)
-    for copy in small:
-        copy.wait()
-    a_g, a_u = ag[...].astype(F32), au[...].astype(F32)
-    first[col] = jnp.concatenate([a_g[0:2], a_u[0:2], a_g[2:4], a_u[2:4]], 0).astype(BF16)
-    b_rows = jnp.concatenate([bg[...].astype(F32), bu[...].astype(F32)], 0)
-    b_tail = jnp.concatenate([b_rows[:, PART:], jnp.zeros((4, 2 * PART - UNITS), F32)], 1)
-    slot_b = core * 16 + x * 4 + z
-    second[slot_b] = jnp.concatenate([b_rows[:, :PART], b_tail], 0).astype(BF16)
     pl.semaphore_wait(barrier, len(partners))
 
     started = []
@@ -139,9 +131,17 @@
         ref = first.at[y * 2 + side]
         return send_each(7, lambda i: (ref, ref, device(y=(y + 1 + i) % 8)))
 
-    a_zh = [send(first.at[col], first.at[col], zh_peer)]
     tok_zh = [send(tok_hbm, block(zh, 0), zh_peer)]
     tok_in = [spread_tokens(zh, tok_hbm), None]
+    for copy in small:
+        copy.wait()
+    a_g, a_u = ag[...].astype(F32), au[...].astype(F32)
+    first[col] = jnp.concatenate([a_g[0:2], a_u[0:2], a_g[2:4], a_u[2:4]], 0).astype(BF16)
+    b_rows = jnp.concatenate([bg[...].astype(F32), bu[...].astype(F32)], 0)
+    b_tail = jnp.concatenate([b_rows[:, PART:], jnp.zeros((4, 2 * PART - UNITS), F32)], 1)
+    slot_b = core * 16 + x * 4 + z
+    second[slot_b] = jnp.concatenate([b_rows[:, :PART], b_tail], 0).astype(BF16)
+    a_zh = [send(first.at[col], first.at[col], zh_peer)]
     a_own_in = spread_first(zh)
     b_own = second.at[slot_b]
     b_in = send_each(3, lambda i: (b_own, b_own, device(z=(z + 1 + i) % 4)))
@@ -318,7 +318,7 @@
     y1, y2, y34 = {}, {}, {}
 
     def step_down(q):
-        if q == 0:
+        if q == 1:
             down.wait()
         down_half(q, core)
         arrived([core_g[q, 0], core_g[q, 1]])
@@ -359,10 +359,10 @@
         return total + y2_in[q, 0].astype(F32) + y2_in[q, 1].astype(F32)
 
     tok_in[0] = relay_tokens(zh, tok_in[0])
+    arrived(tok_zh)
+    tok_in[1] = spread_tokens(1 - zh, block(1 - zh, 0))
     arrived(a_zh)
     a_other_in = spread_first(1 - zh)
-    arrived(tok_zh)
-    tok_in[1] = spread_tokens(1 - zh, block(1 - zh, 0))
     b_in()
     b_x = second.at[pl.ds(core * 16 + x * 4, 4)]
     b_in = send_each(3, lambda i: (b_x, b_x, device(x=(x + 1 + i) % 4)))
@@ -371,50 +371,50 @@
     weights[1].wait()
     arrived(tok_in[0])
     step_project(0, 0)
+    tok_in[1] = relay_tokens(1 - zh, tok_in[1])
     a_own_in()
     a_other_in()
     first_flat[...] = first[...].astype(F32).reshape(RANKS, FEAT).astype(BF16)
     step_project(0, 1)
-    step_x1(0, 0)
-    tok_in[1] = relay_tokens(1 - zh, tok_in[1])
     step_x1(0, 1)
+    arrived(tok_in[1])
+    step_project(1, 1)
+    step_project(1, 0)
     b_in()
     b_core = second.at[pl.ds(core * 16, 16)]
     b_in = [send(b_core, b_core, core_peer)]
-    arrived(tok_in[1])
-    step_project(1, 1)
-    step_project(1, 0)
-    step_x2(0, 0)
     step_x1(1, 1)
     step_x2(0, 1)
     step_x1(1, 0)
-    step_z(0, 0)
+    step_z(0, 1)
     arrived(b_in)
     second_flat[...] = second[...].astype(F32).reshape(256, PART).astype(BF16)
     step_x2(1, 1)
-    step_z(0, 1)
+    step_x1(0, 0)
     step_x2(1, 0)
     step_hidden(0, 1)
-    step_hidden(0, 0)
     step_z(1, 1)
+    step_z(1, 0)
     step_xg(0, 1)
-    step_z(1, 0)
-    step_xg(0, 0)
+    step_x2(0, 0)
     step_hidden(1, 1)
+    step_hidden(1, 0)
+    step_z(0, 0)
     step_core_g(0, 1)
-    step_hidden(1, 0)
-    step_core_g(0, 0)
     step_xg(1, 1)
     step_xg(1, 0)
-    step_down(0)
+    step_hidden(0, 0)
     step_core_g(1, 1)
     step_core_g(1, 0)
-    step_y2(0)
+    step_xg(0, 0)
     step_down(1)
-    own = y_sum(0)
+    step_core_g(0, 0)
     step_y2(1)
+    step_down(0)
     last_out[...] = y_sum(1).astype(BF16)
     final = send(last_out, last_in, zh_peer)
+    step_y2(0)
+    own = y_sum(0)
     arrived([final])
     o_ref[...] = (own + last_in[...].astype(F32)).astype(BF16)
     for copy in started:

time: 81.5 us -> 78.6 us (0.964); the launches traced: 80.4 us -> 78.4 us
  Pallas kernels: 79 us -> 77 us
    pallas_call x1, Pallas kernels: 79 us -> 77 us  [per_device(): pl.pallas_call(kernel, out_shape=jax.ShapeDtypeStruct((32, OUT), BF16), i...]
where the time goes in v4:
time: 78.6 us; the launch traced here: 78.4 us
  Pallas kernels  77 us (98%)
  local copies, waits for them, and re-layouts  1.38 us (2%)
    pallas_call x1, Pallas kernels, per_device(): pl.pallas_call(kernel, out_shape=jax.ShapeDtypeStruct((32, OUT), BF16), i...  77 us

profile of v4, /device:TPU:1, one launch (start us, length us, event | category | flops | bytes accessed | tf_op | source)
XLA Modules:
  0.0 78.4 jit_solution(8967006670598750507)
XLA Ops:
  0.0 77.0 %ffn.1 = bf16[32,512]{1,0:T(8,128)(2,1)} custom-call(bf16[32,512]{1,0:T(8,128)(2,1)} %tok_hbm.1, bf16[512,1664]{1,0:T(8,128)(2,1)} %gw_hbm.1, bf16[512,1664]{1,0:T(8,128)(2,1)} %uw_hbm.1, bf16[1664,512]{1,0:T(8,128)(2,1)} %dw_hbm.1, bf16[4,512]{1,0:T(4,128)(2,1)} %bitcast.2, bf16[2,1664]{1,0:T(2,128)(2,1)} %bg_hbm.1, bf16[4,512]{1,0:T(4,128)(2,1)} %bitcast.3, ...), custom_call_target="tpu_custom_call" | custom-call | tf_op jit(solution)/shard_map/ffn/pallas_call | solution.py:430
  77.0 1.4 %copy.10 = bf16[32,512]{1,0:T(8,128)(2,1)} copy(bf16[32,512]{1,0:T(8,128)(2,1)} %ffn.1) | data formatting | bytes 65536
